TPU v7x, 256 devices: a whole 4x4x8 slice. The times are simulated.
256 devices in a mesh: dp: 2 (over x_lo), ctx: 32 (over z, y), tp: 4 (over x_hi, core).
Axes of the slice: x: 4 (x_hi: 2, x_lo: 2; x = x_hi * 2 + x_lo), y: 4, z: 8, core: 2. Of those that a mesh axis runs over, the one named last changes fastest.
Arguments:
- query_proj: bfloat16 [2, 8192, 2048], P('dp', 'ctx', 'tp'), may hold values from -6 to 6
- key_proj: bfloat16 [2, 8192, 2048], P('dp', 'ctx', 'tp'), may hold values from -6 to 6
- value_proj: bfloat16 [2, 8192, 2048], P('dp', 'ctx', 'tp'), may hold values from -6 to 6
- filters: float32 [2048, 8192], P('tp', 'ctx'), may hold values from -2 to 2
- w_out: bfloat16 [2048, 2048], P('tp'), may hold values from -0.125 to 0.125
- cotangent: bfloat16 [2, 8192, 2048], P('dp', 'ctx', 'tp'), may hold values from -6 to 6
Outputs:
- output: bfloat16 [2, 8192, 2048], P('dp', 'ctx', 'tp')
- grad_query: bfloat16 [2, 8192, 2048], P('dp', 'ctx', 'tp')
- grad_key: bfloat16 [2, 8192, 2048], P('dp', 'ctx', 'tp')
- grad_value: bfloat16 [2, 8192, 2048], P('dp', 'ctx', 'tp')
- grad_filter: float32 [2048, 8192], P('tp', 'ctx')
- grad_wout: float32 [2048, 2048], P('tp', 'ctx')
All inputs are finite; a program needn't handle non-finite values.
Results may differ from a plain program's by a relative error of at most 0.0049.
Values may be sent and summed in bfloat16 or wider, within the bound.
A program may use at most 64 MiB of HBM per device.

v0:
```python
import functools
import math

import jax
import jax.numpy as jnp
import ml_dtypes
import numpy as np
from jax import lax
from jax.experimental import pallas as pl
from jax.experimental.pallas import tpu as pltpu
from jax.sharding import PartitionSpec as P

MESH = pl.DeviceIdType.MESH
F32 = jnp.float32
BF16 = jnp.bfloat16

DP = 2
SEQ = 32
ZN = 8
YN = 4
GROUP = DP * SEQ
CH = 8
BLOCKS = 64
LANES = 128
LENGTH = BLOCKS * LANES
ROWS = BLOCKS * CH
STEP = 256


def halves(table):
    high = table.astype(ml_dtypes.bfloat16)
    low = (table - high.astype(np.float64)).astype(ml_dtypes.bfloat16)
    return np.stack([high, low])


@functools.lru_cache(maxsize=None)
def tables():
    k1 = np.arange(BLOCKS)[:, None].astype(np.float64)
    turn = 2 * math.pi * k1 + math.pi / 2
    outer = turn * np.arange(BLOCKS)[None, :] / BLOCKS
    eye = np.eye(CH)
    stage_one = np.concatenate([np.kron(np.cos(outer), eye), np.kron(-np.sin(outer), eye)], axis=0)
    angle = np.repeat(turn * np.arange(LANES)[None, :] / LENGTH, CH, axis=0)
    twiddle = np.stack([np.cos(angle), -np.sin(angle)]).astype(np.float32)
    lane = np.arange(LANES)
    inner = 2 * math.pi * ((lane[:, None] * lane[None, :]) % LANES) / LANES
    c, s = np.cos(inner), np.sin(inner)
    stage_two = np.block([[c, -s], [s, c]])
    stage_two_back = np.block([[c, s], [-s, c]])
    return (
        halves(stage_one),
        halves(stage_one.T),
        np.concatenate([halves(stage_two), halves(stage_two_back)]),
        twiddle,
    )


def dot(a, b):
    return jnp.dot(a, b, preferred_element_type=F32)


def split(x):
    high = x.astype(BF16)
    return high, (x - high.astype(F32)).astype(BF16)


def kernel(
    factor,
    q_ref, k_ref, v_ref, f_ref, w_ref, cot_ref, one_hbm, back_hbm, two_hbm, tw_hbm,
    out_ref, gq_ref, gk_ref, gv_ref, gf_ref, gw_ref,
    one, back, two, tw,
    mix_send, mix_recv, fil_send, fil_recv, gc_send, gc_recv,
    conv_send, conv_recv, gm_send, gm_recv, fg_send, fg_recv,
    cot_all, cot_t, gg, xcat, spec_m, spec_f, spec_g, v_hi, v_lo,
    gated, w_send, w_recv, z_send, z_recv, d_send, d_recv,
    core_send, core_recv, x_send, x_recv, own,
    table_sem, send_sem, recv_sem, tp_send, tp_recv, y_ssem, y_rsem, z_ssem, z_rsem, d_sem,
):
    d = lax.axis_index("dp")
    j = lax.axis_index("ctx")
    t = lax.axis_index("tp")
    z = j // YN
    y = lax.rem(j, YN)
    core = lax.rem(t, 2)
    hi_x = t // 2
    me = d * SEQ + j
    t_core = hi_x * 2 + (1 - core)
    t_x = (1 - hi_x) * 2 + core
    t_far = (1 - hi_x) * 2 + (1 - core)

    def peer(offset):
        p = lax.rem(me + offset, GROUP)
        return p, {"dp": p // SEQ, "ctx": lax.rem(p, SEQ)}

    local = []
    for i, (src, dst) in enumerate(((one_hbm, one), (two_hbm, two), (tw_hbm, tw), (back_hbm, back))):
        copy = pltpu.make_async_copy(src, dst, table_sem.at[i])
        copy.start()
        local.append(copy)

    barrier = pltpu.get_barrier_semaphore()

    def greet(i, carry):
        pl.semaphore_signal(barrier, inc=1, device_id=peer(i)[1], device_id_type=MESH)
        return carry

    lax.fori_loop(1, GROUP, greet, 0)
    for other in (t_core, t_x):
        pl.semaphore_signal(barrier, inc=1, device_id={"tp": other}, device_id_type=MESH)

    def to_chunks(rows):
        count = rows.shape[0] // CH
        parts = [rows[:, h * LANES : (h + 1) * LANES].reshape(count, CH, LANES) for h in range(2)]
        return jnp.concatenate(parts, axis=1).astype(BF16)

    def from_chunks(ref):
        chunks = ref[...].astype(F32)
        parts = [chunks[:, h * CH : (h + 1) * CH, :].reshape(GROUP * CH, LANES) for h in range(2)]
        return jnp.concatenate(parts, axis=1)

    mix_send[...] = to_chunks((k_ref[...].astype(F32) * v_ref[...].astype(F32)).T)
    half = SEQ * CH
    fil_send[...] = to_chunks(f_ref[pl.ds(pl.multiple_of(d * half, half), half), :])
    mix_recv[me] = mix_send[me]
    fil_recv[j] = fil_send[j]
    cot_all[t] = cot_ref[...]

    pl.semaphore_wait(barrier, GROUP + 1)

    def remote(src, dst, ssem, rsem, device):
        return pltpu.make_async_remote_copy(
            src_ref=src, dst_ref=dst, send_sem=ssem, recv_sem=rsem, device_id=device, device_id_type=MESH
        )

    cot_core = remote(cot_ref, cot_all.at[t], tp_send.at[0], tp_recv.at[0], {"tp": t_core})
    cot_x = remote(cot_ref, cot_all.at[t], tp_send.at[1], tp_recv.at[1], {"tp": t_x})
    cot_x.start()
    cot_core.start()

    def scatter(src, dst, index, same):
        def start(i, carry):
            p, device = peer(i)
            chunk = lax.rem(p, SEQ) if same else p
            remote(src.at[chunk], dst.at[me], send_sem.at[index], recv_sem.at[index], device).start()
            return carry

        lax.fori_loop(1, GROUP, start, 0)

    def arrived(dst, index, count=GROUP - 1):
        part = dst.at[pl.ds(0, count)]
        remote(part, part, send_sem.at[index], recv_sem.at[index], {"tp": t_core}).wait_recv()

    def left(dst, index, count=GROUP - 1):
        part = dst.at[pl.ds(0, count)]
        remote(part, part, send_sem.at[index], recv_sem.at[index], {"tp": t_core}).wait_send()

    scatter(mix_send, mix_recv, 0, False)

    def start_filter(i, carry):
        p = lax.rem(j + i, SEQ)
        remote(fil_send.at[p], fil_recv.at[j], send_sem.at[1], recv_sem.at[1], {"ctx": p}).start()
        return carry

    lax.fori_loop(1, SEQ, start_filter, 0)

    width = cot_ref.shape[1]

    def grad_part(o):
        weights = w_ref[:, pl.ds(pl.multiple_of(o * width, width), width)]
        return lax.dot_general(
            cot_all[o], weights, (((1,), (1,)), ((), ())), preferred_element_type=F32
        )

    def turn(o):
        rows = pl.ds(pl.multiple_of(o * width, width), width)
        cot_t[rows, :] = cot_all[o].astype(F32).T.astype(BF16)

    gg[...] = grad_part(t)
    turn(t)
    cot_core.wait_recv()
    gg[...] += grad_part(t_core)
    turn(t_core)
    cot_x.wait_recv()
    forward = remote(
        cot_all.at[t_x], cot_all.at[t_x], tp_send.at[2], tp_recv.at[2], {"tp": t_core}
    )
    forward.start()
    gg[...] += grad_part(t_x)
    forward.wait_recv()
    total = gg[...] + grad_part(t_far)
    gg[...] = total
    gc_send[...] = to_chunks((total * q_ref[...].astype(F32)).T)
    gc_recv[me] = gc_send[me]
    scatter(gc_send, gc_recv, 2, False)
    turn(t_x)
    turn(t_far)

    def rows_of(i, base=0):
        return pl.ds(pl.multiple_of(base + i * STEP, STEP), STEP)

    def forward_transform(recv, count, spec):
        for b in range(count):
            xcat[:, b * LANES : (b + 1) * LANES] = recv[b * SEQ : (b + 1) * SEQ].reshape(ROWS, LANES)

        def body(i, carry):
            x = xcat[:, : count * LANES]
            real = dot(one[0, rows_of(i), :], x) + dot(one[1, rows_of(i), :], x)
            imag = dot(one[0, rows_of(i, ROWS), :], x) + dot(one[1, rows_of(i, ROWS), :], x)
            c, s = tw[0, rows_of(i), :], tw[1, rows_of(i), :]
            for b in range(count):
                re = real[:, b * LANES : (b + 1) * LANES]
                im = imag[:, b * LANES : (b + 1) * LANES]
                high, low = split(jnp.concatenate([re * c - im * s, re * s + im * c], axis=1))
                spec[b, rows_of(i), :] = dot(high, two[0]) + dot(low, two[0]) + dot(high, two[1])
            return carry

        lax.fori_loop(0, ROWS // STEP, body, 0)

    def inverse_transform(product, count, send):
        def first(i, carry):
            c, s = tw[0, rows_of(i), :], tw[1, rows_of(i), :]
            for b in range(count):
                high, low = split(jnp.concatenate(product(b, rows_of(i)), axis=1))
                u = dot(high, two[2]) + dot(low, two[2]) + dot(high, two[3])
                re, im = u[:, :LANES], u[:, LANES:]
                lanes = slice(b * LANES, (b + 1) * LANES)
                high, low = split(re * c + im * s)
                v_hi[rows_of(i), lanes] = high
                v_lo[rows_of(i), lanes] = low
                high, low = split(im * c - re * s)
                v_hi[rows_of(i, ROWS), lanes] = high
                v_lo[rows_of(i, ROWS), lanes] = low
            return carry

        lax.fori_loop(0, ROWS // STEP, first, 0)

        def second(i, carry):
            high, low = v_hi[:, : count * LANES], v_lo[:, : count * LANES]
            table = back[0, rows_of(i), :]
            result = dot(table, high) + dot(table, low) + dot(back[1, rows_of(i), :], high)
            result = (result * (1.0 / LENGTH)).astype(BF16)
            chunks = STEP // (2 * CH)
            for b in range(count):
                part = result[:, b * LANES : (b + 1) * LANES].reshape(chunks, 2 * CH, LANES)
                send[pl.ds(b * SEQ + i * chunks, chunks)] = part
            return carry

        lax.fori_loop(0, ROWS // STEP, second, 0)

    def pair(ref, b, rows):
        return ref[b, rows, :LANES], ref[b, rows, LANES:]

    def conv_product(b, rows):
        fr, fi = pair(spec_f, 0, rows)
        mr, mi = pair(spec_m, b, rows)
        return fr * mr - fi * mi, fr * mi + fi * mr

    def grad_product(b, rows):
        fr, fi = pair(spec_f, 0, rows)
        gr, gi = pair(spec_g, b, rows)
        return fr * gr + fi * gi, fr * gi - fi * gr

    def taps_product(_, rows):
        real, imag = 0.0, 0.0
        for b in range(DP):
            mr, mi = pair(spec_m, b, rows)
            gr, gi = pair(spec_g, b, rows)
            real += gr * mr + gi * mi
            imag += gi * mr - gr * mi
        return real, imag

    for copy in local:
        copy.wait()
    arrived(mix_recv, 0)
    forward_transform(mix_recv, DP, spec_m)
    arrived(fil_recv, 1, SEQ - 1)
    forward_transform(fil_recv, 1, spec_f)
    inverse_transform(conv_product, DP, conv_send)
    conv_recv[me] = conv_send[me]
    scatter(conv_send, conv_recv, 3, False)
    arrived(gc_recv, 2)
    forward_transform(gc_recv, DP, spec_g)
    inverse_transform(grad_product, DP, gm_send)
    gm_recv[me] = gm_send[me]
    scatter(gm_send, gm_recv, 4, False)
    inverse_transform(taps_product, 1, fg_send)
    fg_recv[me] = fg_send[j]
    scatter(fg_send, fg_recv, 5, True)

    arrived(conv_recv, 3)
    conv = from_chunks(conv_recv).T
    gq_ref[...] = (gg[...] * conv).astype(BF16)
    gated[...] = (q_ref[...].astype(F32) * conv).astype(BF16)

    features = gw_ref.shape[1]
    channels = gw_ref.shape[0]
    for o in range(4):
        term = dot(cot_t[o * width : (o + 1) * width, :], gated[...])
        for piece in range(width // features):
            part = term[piece * features : (piece + 1) * features, :].astype(BF16)
            w_send[piece % YN, o * 2 + piece // YN] = part
    y_copies = []
    for step in (2, 1, 3):
        to = lax.rem(y + step, YN)
        copy = remote(
            w_send.at[to], w_recv.at[step - 1], y_ssem.at[step - 1], y_rsem.at[step - 1],
            {"ctx": z * YN + to},
        )
        copy.start()
        y_copies.append(copy)

    def partial(o):
        return dot(gated[...], w_ref[:, pl.ds(pl.multiple_of(o * width, width), width)])

    core_send[0] = partial(t_far)
    core_send[1] = partial(t_core)
    core_copy = remote(core_send, core_recv, tp_send.at[3], tp_recv.at[3], {"tp": t_core})
    core_copy.start()
    other_x = partial(t_x)
    own[...] = partial(t)
    core_copy.wait_recv()
    x_send[...] = (other_x + core_recv[0]).astype(BF16)
    x_copy = remote(x_send, x_recv, tp_send.at[4], tp_recv.at[4], {"tp": t_x})
    x_copy.start()

    arrived(gm_recv, 4)
    grad_mixed = from_chunks(gm_recv).T
    gk_ref[...] = (grad_mixed * v_ref[...].astype(F32)).astype(BF16)
    gv_ref[...] = (grad_mixed * k_ref[...].astype(F32)).astype(BF16)
    arrived(fg_recv, 5)
    gf_ref[...] = from_chunks(fg_recv) * factor

    x_copy.wait_recv()
    out_ref[...] = (own[...] + core_recv[1] + x_recv[...].astype(F32)).astype(BF16)

    for copy in y_copies:
        copy.wait_recv()

    def reduce_y(i, carry):
        value = w_send[y, i].astype(F32)
        for slot in range(YN - 1):
            value += w_recv[slot, i].astype(F32)
        z_send[i] = value.astype(BF16)
        return carry

    lax.fori_loop(0, ZN, reduce_y, 0)
    z_recv[z] = z_send[z]
    z_copies = []
    for step in (4, 3, 5, 2, 6, 1, 7):
        to = lax.rem(z + step, ZN)
        copy = remote(
            z_send.at[to], z_recv.at[z], z_ssem.at[step - 1], z_rsem.at[step - 1],
            {"ctx": to * YN + y},
        )
        copy.start()
        z_copies.append(copy)
    for copy in z_copies:
        copy.wait_recv()
    value = z_recv[0].astype(F32)
    for slot in range(1, ZN):
        value += z_recv[slot].astype(F32)
    d_send[...] = value
    d_copy = remote(d_send, d_recv, d_sem.at[0], d_sem.at[1], {"dp": 1 - d})
    d_copy.start()
    d_copy.wait_recv()
    gw_ref[...] = ((d_send[...] + d_recv[...]) * factor).T

    for copy in (cot_core, cot_x, forward, core_copy, x_copy, d_copy, *y_copies, *z_copies):
        copy.wait_send()
    left(mix_send, 0)
    left(fil_send, 1, SEQ - 1)
    left(gc_send, 2)
    left(conv_send, 3)
    left(gm_send, 4)
    left(fg_recv, 5)


def local(query_proj, key_proj, value_proj, filters, w_out, cotangent):
    positions, channels = query_proj.shape[1:]
    features = w_out.shape[1] // SEQ
    factor = 1.0 / math.sqrt(DP * LENGTH)
    one, back, two, twiddle = (jnp.asarray(table) for table in tables())
    stream = jax.ShapeDtypeStruct((positions, channels), BF16)
    vmem = pl.BlockSpec(memory_space=pltpu.VMEM)
    anywhere = pl.BlockSpec(memory_space=pl.ANY)
    chunks = pltpu.VMEM((GROUP, 2 * CH, LANES), BF16)
    half_chunks = pltpu.VMEM((SEQ, 2 * CH, LANES), BF16)
    wide = w_out.shape[1]
    dma = pltpu.SemaphoreType.DMA
    outs = pl.pallas_call(
        functools.partial(kernel, factor),
        out_shape=(
            stream,
            stream,
            stream,
            stream,
            jax.ShapeDtypeStruct((channels, positions), F32),
            jax.ShapeDtypeStruct((channels, features), F32),
        ),
        in_specs=[vmem] * 6 + [anywhere] * 4,
        out_specs=[vmem] * 6,
        scratch_shapes=[
            pltpu.VMEM(one.shape, BF16),
            pltpu.VMEM(back.shape, BF16),
            pltpu.VMEM(two.shape, BF16),
            pltpu.VMEM(twiddle.shape, F32),
            chunks, chunks, half_chunks, half_chunks, chunks, chunks,
            chunks, chunks, chunks, chunks, half_chunks, chunks,
            pltpu.VMEM((4, positions, channels), BF16),
            pltpu.VMEM((wide, positions), BF16),
            pltpu.VMEM((positions, channels), F32),
            pltpu.VMEM((ROWS, DP * LANES), BF16),
            pltpu.VMEM((DP, ROWS, 2 * LANES), F32),
            pltpu.VMEM((1, ROWS, 2 * LANES), F32),
            pltpu.VMEM((DP, ROWS, 2 * LANES), F32),
            pltpu.VMEM((2 * ROWS, DP * LANES), BF16),
            pltpu.VMEM((2 * ROWS, DP * LANES), BF16),
            pltpu.VMEM((positions, channels), BF16),
            pltpu.VMEM((YN, ZN, features, channels), BF16),
            pltpu.VMEM((YN - 1, ZN, features, channels), BF16),
            pltpu.VMEM((ZN, features, channels), BF16),
            pltpu.VMEM((ZN, features, channels), BF16),
            pltpu.VMEM((features, channels), F32),
            pltpu.VMEM((features, channels), F32),
            pltpu.VMEM((2, positions, channels), F32),
            pltpu.VMEM((2, positions, channels), F32),
            pltpu.VMEM((positions, channels), BF16),
            pltpu.VMEM((positions, channels), BF16),
            pltpu.VMEM((positions, channels), F32),
            dma((4,)), dma((6,)), dma((6,)), dma((5,)), dma((5,)),
            dma((3,)), dma((3,)), dma((7,)), dma((7,)), dma((2,)),
        ],
        compiler_params=pltpu.CompilerParams(
            collective_id=0, has_side_effects=True, vmem_limit_bytes=56 * 1024 * 1024
        ),
        cost_estimate=pl.CostEstimate(flops=8_000_000_000, bytes_accessed=12_000_000, transcendentals=0),
    )(query_proj[0], key_proj[0], value_proj[0], filters, w_out, cotangent[0], one, back, two, twiddle)
    output, grad_query, grad_key, grad_value, grad_filter, grad_wout = outs
    return (
        output[None],
        grad_query[None],
        grad_key[None],
        grad_value[None],
        grad_filter,
        grad_wout,
    )


def solution(mesh):
    stream = P("dp", "ctx", "tp")
    taps = P("tp", "ctx")
    return jax.shard_map(
        local,
        mesh=mesh,
        in_specs=(stream, stream, stream, taps, P("tp", None), stream),
        out_specs=(stream, stream, stream, stream, taps, taps),
        check_vma=False,
    )
```

profile of v0, /device:TPU:1, one launch (start us, length us, event | category | flops | bytes accessed | tf_op | source)
XLA Modules:
  0.0 101.4 jit_solution(11797678455506754643)
XLA Ops:
  0.6 92.4 %shard_map.145 = (bf16[256,512]{1,0:T(8,128)(2,1)}, bf16[256,512]{1,0:T(8,128)(2,1)}, bf16[256,512]{1,0:T(8,128)(2,1)}, bf16[256,512]{1,0:T(8,128)(2,1)}, f32[512,256]{1,0:T(8,128)}, /*index=5*/f32[512,64]{1,0:T(8,128)}) custom-call(bf16[256,512]{1,0:T(8,128)(2,1)} %bitcast.12, bf16[256,512]{1,0:T(8,128)(2,1)} %bitcast.13, bf16[256,512]{1,0:T(8,128)(2,1)} %bitcast.14, ...), custom_call_target="tpu_custom_call" | custom-call | flops 8000000000 | bytes 12000000 | tf_op jit(solution)/shard_map/pallas_call | solution.py:390
  93.1 0.0 copy-start.1
  93.1 0.0 copy-start
  93.1 1.8 %copy.16 = f32[512,64]{0,1:T(8,128)} copy(f32[512,64]{1,0:T(8,128)} %get-tuple-element.23) | data formatting | bytes 262144
  94.9 1.7 %copy.22 = bf16[1,256,512]{2,1,0:T(8,128)(2,1)} copy(bf16[1,256,512]{2,1,0:T(8,128)(2,1)} %bitcast.11) | data formatting | bytes 524288
  96.5 1.7 %copy.23 = bf16[1,256,512]{2,1,0:T(8,128)(2,1)} copy(bf16[1,256,512]{2,1,0:T(8,128)(2,1)} %bitcast.10) | data formatting | bytes 524288
  98.2 1.7 %copy.24 = bf16[1,256,512]{2,1,0:T(8,128)(2,1)} copy(bf16[1,256,512]{2,1,0:T(8,128)(2,1)} %bitcast.9) | data formatting | bytes 524288
  99.9 0.0 copy-done.1
  99.9 0.7 copy.25
  100.6 0.0 copy-done
  100.6 0.8 copy.26
Async XLA Ops:
  93.1 6.8 %copy-start.1 = (bf16[256,512]{1,0:T(8,128)(2,1)S(1)}, bf16[256,512]{1,0:T(8,128)(2,1)}, u32[]{:S(2)}) copy-start(bf16[256,512]{1,0:T(8,128)(2,1)} %get-tuple-element.15) | copy-start | bytes 786436
  93.1 7.5 %copy-start = (f32[512,256]{1,0:T(8,128)S(1)}, f32[512,256]{1,0:T(8,128)}, u32[]{:S(2)}) copy-start(f32[512,256]{1,0:T(8,128)} %get-tuple-element.34) | copy-start | bytes 1572868
where the time goes:
time: 102 us; the launch traced here: 101 us
  Pallas kernels  92.4 us (91%)
  local copies, waits for them, and re-layouts  8.3 us (8%)
    pallas_call x1, Pallas kernels, local(): pl.pallas_call(functools.partial(kernel, factor), out_shape=(stream, stre...  92.4 us
    unnamed x10, local copies, waits for them, and re-layouts  8.3 us

commit v1 on v0

v1 whole, which is shorter than its diff:
```python
import functools
import math

import jax
import jax.numpy as jnp
import ml_dtypes
import numpy as np
from jax import lax
from jax.experimental import pallas as pl
from jax.experimental.pallas import tpu as pltpu
from jax.sharding import PartitionSpec as P

MESH = pl.DeviceIdType.MESH
F32 = jnp.float32
BF16 = jnp.bfloat16

DP = 2
SEQ = 32
ZN = 8
YN = 4
GROUP = DP * SEQ
CH = 8
BLOCKS = 64
LANES = 128
LENGTH = BLOCKS * LANES
ROWS = BLOCKS * CH
STEP = 256


def halves(table):
    high = table.astype(ml_dtypes.bfloat16)
    low = (table - high.astype(np.float64)).astype(ml_dtypes.bfloat16)
    return np.stack([high, low])


@functools.lru_cache(maxsize=None)
def tables():
    k1 = np.arange(BLOCKS)[:, None].astype(np.float64)
    turn = 2 * math.pi * k1 + math.pi / 2
    outer = turn * np.arange(BLOCKS)[None, :] / BLOCKS
    eye = np.eye(CH)
    stage_one = np.concatenate([np.kron(np.cos(outer), eye), np.kron(-np.sin(outer), eye)], axis=0)
    angle = np.repeat(turn * np.arange(LANES)[None, :] / LENGTH, CH, axis=0)
    twiddle = np.stack([np.cos(angle), -np.sin(angle)]).astype(np.float32)
    lane = np.arange(LANES)
    inner = 2 * math.pi * ((lane[:, None] * lane[None, :]) % LANES) / LANES
    c, s = np.cos(inner), np.sin(inner)
    stage_two = np.block([[c, -s], [s, c]])
    stage_two_back = np.block([[c, s], [-s, c]])
    return (
        halves(stage_one),
        halves(stage_one.T),
        np.concatenate([halves(stage_two), halves(stage_two_back)]),
        twiddle,
    )


def dot(a, b):
    return jnp.dot(a, b, preferred_element_type=F32)


def split(x):
    high = x.astype(BF16)
    return high, (x - high.astype(F32)).astype(BF16)


def kernel(
    factor,
    q_hbm, k_hbm, v_hbm, f_hbm, w_hbm, cot_hbm, one_hbm, back_hbm, two_hbm, tw_hbm,
    out_hbm, gq_hbm, gk_hbm, gv_hbm, gf_hbm, gw_hbm,
    q_ref, k_ref, v_ref, f_ref, w_ref,
    out_ref, gq_ref, gk_ref, gv_ref, gf_ref, gw_ref,
    one, back, two, tw,
    mix_send, mix_recv, fil_send, fil_recv, gc_send, gc_recv,
    conv_send, conv_recv, gm_send, gm_recv, fg_send, fg_recv, fg_part,
    cot_all, cot_t, cot_p, gg, xcat, spec_m, spec_f, spec_g, v_hi, v_lo,
    gated, gated_p, w_send, w_recv, z_send, z_recv, d_send, d_recv,
    core_send, core_recv, x_send, x_recv, own,
    load_sem, store_sem, send_sem, recv_sem, tp_send, tp_recv, dp_send, dp_recv,
    y_ssem, y_rsem, z_ssem, z_rsem,
):
    d = lax.axis_index("dp")
    j = lax.axis_index("ctx")
    t = lax.axis_index("tp")
    z = j // YN
    y = lax.rem(j, YN)
    core = lax.rem(t, 2)
    hi_x = t // 2
    me = d * SEQ + j
    t_core = hi_x * 2 + (1 - core)
    t_x = (1 - hi_x) * 2 + core
    t_far = (1 - hi_x) * 2 + (1 - core)

    def peer(offset):
        p = lax.rem(me + offset, GROUP)
        return p, {"dp": p // SEQ, "ctx": lax.rem(p, SEQ)}

    barrier = pltpu.get_barrier_semaphore()

    def greet(i, carry):
        pl.semaphore_signal(barrier, inc=1, device_id=peer(i)[1], device_id_type=MESH)
        return carry

    def load(src, dst, index):
        copy = pltpu.make_async_copy(src, dst, load_sem.at[index])
        copy.start()
        return copy

    def store(src, dst, index):
        copy = pltpu.make_async_copy(src, dst, store_sem.at[index])
        copy.start()
        return copy

    load_f = load(f_hbm, f_ref, 0)
    load_k = load(k_hbm, k_ref, 1)
    load_v = load(v_hbm, v_ref, 2)
    load_cot = load(cot_hbm, cot_all.at[t], 3)
    lax.fori_loop(1, GROUP, greet, 0)
    for other in (t_core, t_x):
        pl.semaphore_signal(barrier, inc=1, device_id={"tp": other}, device_id_type=MESH)
    load_w = load(w_hbm, w_ref, 4)
    load_q = load(q_hbm, q_ref, 5)
    load_tables = [
        load(src, dst, 6 + i)
        for i, (src, dst) in enumerate(((one_hbm, one), (two_hbm, two), (tw_hbm, tw), (back_hbm, back)))
    ]

    def to_chunks(rows):
        count = rows.shape[0] // CH
        parts = [rows[:, h * LANES : (h + 1) * LANES].reshape(count, CH, LANES) for h in range(2)]
        return jnp.concatenate(parts, axis=1).astype(BF16)

    def from_chunks(ref):
        chunks = ref[...].astype(F32)
        count = chunks.shape[0]
        parts = [chunks[:, h * CH : (h + 1) * CH, :].reshape(count * CH, LANES) for h in range(2)]
        return jnp.concatenate(parts, axis=1)

    half = SEQ * CH
    load_f.wait()
    fil_send[...] = to_chunks(f_ref[pl.ds(pl.multiple_of(d * half, half), half), :])
    fil_recv[j] = fil_send[j]
    load_k.wait()
    load_v.wait()
    mix_send[...] = to_chunks((k_ref[...].astype(F32) * v_ref[...].astype(F32)).T)
    mix_recv[me] = mix_send[me]
    load_cot.wait()

    pl.semaphore_wait(barrier, GROUP + 1)

    def remote(src, dst, ssem, rsem, device):
        return pltpu.make_async_remote_copy(
            src_ref=src, dst_ref=dst, send_sem=ssem, recv_sem=rsem, device_id=device, device_id_type=MESH
        )

    def tp_copy(src, dst, index, to):
        return remote(src, dst, tp_send.at[index], tp_recv.at[index], {"tp": to})

    def dp_copy(src, dst, index):
        return remote(src, dst, dp_send.at[index], dp_recv.at[index], {"dp": 1 - d})

    cot_core = tp_copy(cot_all.at[t], cot_all.at[t], 0, t_core)
    cot_x = tp_copy(cot_all.at[t], cot_all.at[t], 1, t_x)
    cot_x.start()
    cot_core.start()

    def scatter(src, dst, index, first=1, last=GROUP):
        def start(i, carry):
            p, device = peer(i)
            remote(src.at[p], dst.at[me], send_sem.at[index], recv_sem.at[index], device).start()
            return carry

        lax.fori_loop(first, last, start, 0)

    def scatter_same(src, dst, index):
        def start(i, carry):
            p = lax.rem(j + i, SEQ)
            remote(src.at[p], dst.at[j], send_sem.at[index], recv_sem.at[index], {"ctx": p}).start()
            return carry

        lax.fori_loop(1, SEQ, start, 0)

    def whole(ref, index):
        part = ref.at[pl.ds(0, ref.shape[0] - 1)]
        return remote(part, part, send_sem.at[index], recv_sem.at[index], {"tp": t_core})

    scatter_same(fil_send, fil_recv, 1)
    scatter(mix_send, mix_recv, 0)

    width = q_ref.shape[1]
    positions = q_ref.shape[0]
    half_rows = cot_t.shape[2]

    def grad_part(o):
        weights = w_ref[:, pl.ds(pl.multiple_of(o * width, width), width)]
        return lax.dot_general(
            cot_all[o], weights, (((1,), (1,)), ((), ())), preferred_element_type=F32
        )

    per = width // (DP * half_rows)

    def turn(o):
        turned = cot_all[o].astype(F32).T.astype(BF16)
        cot_t[pl.ds(o * per, per)] = turned.reshape(per, DP, half_rows, positions)

    def rows_of(i, base=0):
        return pl.ds(pl.multiple_of(base + i * STEP, STEP), STEP)

    def forward_transform(recv, count, spec):
        for b in range(count):
            xcat[:, b * LANES : (b + 1) * LANES] = recv[b * SEQ : (b + 1) * SEQ].reshape(ROWS, LANES)

        def body(i, carry):
            x = xcat[:, : count * LANES]
            real = dot(one[0, rows_of(i), :], x) + dot(one[1, rows_of(i), :], x)
            imag = dot(one[0, rows_of(i, ROWS), :], x) + dot(one[1, rows_of(i, ROWS), :], x)
            c, s = tw[0, rows_of(i), :], tw[1, rows_of(i), :]
            for b in range(count):
                re = real[:, b * LANES : (b + 1) * LANES]
                im = imag[:, b * LANES : (b + 1) * LANES]
                high, low = split(jnp.concatenate([re * c - im * s, re * s + im * c], axis=1))
                spec[b, rows_of(i), :] = dot(high, two[0]) + dot(low, two[0]) + dot(high, two[1])
            return carry

        lax.fori_loop(0, ROWS // STEP, body, 0)

    def inverse_transform(product, count, send):
        def first(i, carry):
            c, s = tw[0, rows_of(i), :], tw[1, rows_of(i), :]
            for b in range(count):
                high, low = split(jnp.concatenate(product(b, rows_of(i)), axis=1))
                u = dot(high, two[2]) + dot(low, two[2]) + dot(high, two[3])
                re, im = u[:, :LANES], u[:, LANES:]
                lanes = slice(b * LANES, (b + 1) * LANES)
                high, low = split(re * c + im * s)
                v_hi[rows_of(i), lanes] = high
                v_lo[rows_of(i), lanes] = low
                high, low = split(im * c - re * s)
                v_hi[rows_of(i, ROWS), lanes] = high
                v_lo[rows_of(i, ROWS), lanes] = low
            return carry

        lax.fori_loop(0, ROWS // STEP, first, 0)

        def second(i, carry):
            high, low = v_hi[:, : count * LANES], v_lo[:, : count * LANES]
            table = back[0, rows_of(i), :]
            result = dot(table, high) + dot(table, low) + dot(back[1, rows_of(i), :], high)
            result = (result * (1.0 / LENGTH)).astype(BF16)
            chunks = STEP // (2 * CH)
            for b in range(count):
                part = result[:, b * LANES : (b + 1) * LANES].reshape(chunks, 2 * CH, LANES)
                send[pl.ds(b * SEQ + i * chunks, chunks)] = part
            return carry

        lax.fori_loop(0, ROWS // STEP, second, 0)

    def pair(ref, b, rows):
        return ref[b, rows, :LANES], ref[b, rows, LANES:]

    def conv_product(b, rows):
        fr, fi = pair(spec_f, 0, rows)
        mr, mi = pair(spec_m, b, rows)
        return fr * mr - fi * mi, fr * mi + fi * mr

    def grad_product(b, rows):
        fr, fi = pair(spec_f, 0, rows)
        gr, gi = pair(spec_g, b, rows)
        return fr * gr + fi * gi, fr * gi - fi * gr

    def taps_product(_, rows):
        real, imag = 0.0, 0.0
        for b in range(DP):
            mr, mi = pair(spec_m, b, rows)
            gr, gi = pair(spec_g, b, rows)
            real += gr * mr + gi * mi
            imag += gi * mr - gr * mi
        return real, imag

    load_w.wait()
    gg[...] = grad_part(t)
    turn(t)
    cot_core.wait_recv()
    gg[...] += grad_part(t_core)
    turn(t_core)
    for copy in load_tables:
        copy.wait()
    whole(fil_recv, 1).wait_recv()
    forward_transform(fil_recv, 1, spec_f)
    cot_x.wait_recv()
    forward = tp_copy(cot_all.at[t_x], cot_all.at[t_x], 2, t_core)
    forward.start()
    gg[...] += grad_part(t_x)
    load_q.wait()
    forward.wait_recv()
    total = gg[...] + grad_part(t_far)
    gg[...] = total
    gc_send[...] = to_chunks((total * q_ref[...].astype(F32)).T)
    gc_recv[me] = gc_send[me]
    scatter(gc_send, gc_recv, 2, 1, GROUP // 2)
    turn(t_x)
    turn(t_far)
    cot_pair = dp_copy(cot_t.at[:, 1 - d], cot_p, 0)
    cot_pair.start()

    whole(mix_recv, 0).wait_recv()
    forward_transform(mix_recv, DP, spec_m)
    inverse_transform(conv_product, DP, conv_send)
    conv_recv[me] = conv_send[me]
    scatter(conv_send, conv_recv, 3)
    scatter(gc_send, gc_recv, 2, GROUP // 2, GROUP)

    whole(conv_recv, 3).wait_recv()
    conv = from_chunks(conv_recv).T
    gated[...] = (q_ref[...].astype(F32) * conv).astype(BF16)
    gated_pair = dp_copy(gated, gated_p, 1)
    gated_pair.start()
    gq_ref[...] = (gg[...] * conv).astype(BF16)
    stores = [store(gq_ref, gq_hbm, 1)]

    def partial(o):
        return dot(gated[...], w_ref[:, pl.ds(pl.multiple_of(o * width, width), width)])

    core_send[0] = partial(t_far)
    core_send[1] = partial(t_core)
    core_copy = tp_copy(core_send, core_recv, 3, t_core)
    core_copy.start()

    whole(gc_recv, 2).wait_recv()
    forward_transform(gc_recv, DP, spec_g)
    inverse_transform(grad_product, DP, gm_send)
    gm_recv[me] = gm_send[me]
    scatter(gm_send, gm_recv, 4)
    inverse_transform(taps_product, 1, fg_send)
    fg_recv[j] = fg_send[j]
    scatter_same(fg_send, fg_recv, 5)

    cot_pair.wait_recv()
    gated_pair.wait_recv()
    chunks = w_send.shape[0]
    lanes = width // chunks
    planes = ZN // 2
    y_copies = []
    for c in range(chunks):
        cols = slice(c * lanes, (c + 1) * lanes)

        def weight(i, carry, c=c, cols=cols):
            blocks = pl.ds(i * planes * YN, planes * YN)
            mine = cot_t[blocks, d].reshape(planes * YN * half_rows, positions)
            other = cot_p[blocks].reshape(planes * YN * half_rows, positions)
            term = dot(mine, gated[:, cols]) + dot(other, gated_p[:, cols])
            term = term.astype(BF16).reshape(planes, YN, half_rows, lanes)
            for to in range(YN):
                w_send[c, to, pl.ds(i * planes, planes)] = term[:, to]
            return carry

        lax.fori_loop(0, 2, weight, 0)
        for step in (2, 1, 3):
            to = lax.rem(y + step, YN)
            copy = remote(
                w_send.at[c, to], w_recv.at[c, step - 1], y_ssem.at[c, step - 1], y_rsem.at[c, step - 1],
                {"ctx": z * YN + to},
            )
            copy.start()
            y_copies.append(copy)

    other_x = partial(t_x)
    own[...] = partial(t)
    core_copy.wait_recv()
    x_send[...] = (other_x + core_recv[0]).astype(BF16)
    x_copy = tp_copy(x_send, x_recv, 4, t_x)
    x_copy.start()

    z_copies = []

    def reduce_y(c):
        for copy in y_copies[c * 3 : c * 3 + 3]:
            copy.wait_recv()
        value = w_send[c, y].astype(F32)
        for slot in range(YN - 1):
            value += w_recv[c, slot].astype(F32)
        z_send[c] = value.astype(BF16)
        z_recv[c, z] = z_send[c, z]
        for step in (4, 3, 5, 2, 6, 1, 7):
            to = lax.rem(z + step, ZN)
            copy = remote(
                z_send.at[c, to], z_recv.at[c, z], z_ssem.at[c, step - 1], z_rsem.at[c, step - 1],
                {"ctx": to * YN + y},
            )
            copy.start()
            z_copies.append(copy)

    reduce_y(0)
    whole(gm_recv, 4).wait_recv()
    grad_mixed = from_chunks(gm_recv).T
    gk_ref[...] = (grad_mixed * v_ref[...].astype(F32)).astype(BF16)
    gv_ref[...] = (grad_mixed * k_ref[...].astype(F32)).astype(BF16)
    stores += [store(gk_ref, gk_hbm, 2), store(gv_ref, gv_hbm, 3)]
    whole(fg_recv, 5).wait_recv()
    fg_pair = dp_copy(fg_recv, fg_part, 2)
    fg_pair.start()
    for c in range(1, chunks):
        reduce_y(c)
    x_copy.wait_recv()
    out_ref[...] = (own[...] + core_recv[1] + x_recv[...].astype(F32)).astype(BF16)
    stores.append(store(out_ref, out_hbm, 0))
    gf_ref[pl.ds(pl.multiple_of(d * half, half), half), :] = from_chunks(fg_recv) * factor
    fg_pair.wait_recv()
    gf_ref[pl.ds(pl.multiple_of((1 - d) * half, half), half), :] = from_chunks(fg_part) * factor
    stores.append(store(gf_ref, gf_hbm, 4))

    for c in range(chunks):
        for copy in z_copies[c * (ZN - 1) : (c + 1) * (ZN - 1)]:
            copy.wait_recv()
        value = z_recv[c, 0].astype(F32)
        for slot in range(1, ZN):
            value += z_recv[c, slot].astype(F32)
        d_send[:, c * lanes : (c + 1) * lanes] = value * factor
    d_copy = dp_copy(d_send, d_recv, 3)
    d_copy.start()
    gw_ref[pl.ds(pl.multiple_of(d * half_rows, half_rows), half_rows), :] = d_send[...]
    d_copy.wait_recv()
    gw_ref[pl.ds(pl.multiple_of((1 - d) * half_rows, half_rows), half_rows), :] = d_recv[...]
    stores.append(store(gw_ref, gw_hbm, 5))

    for copy in (cot_core, cot_x, forward, core_copy, x_copy, cot_pair, gated_pair, fg_pair, d_copy):
        copy.wait_send()
    for copy in y_copies + z_copies:
        copy.wait_send()
    for index, ref in enumerate((mix_send, fil_send, gc_send, conv_send, gm_send, fg_send)):
        whole(ref, index).wait_send()
    for copy in stores:
        copy.wait()


def hand_over(*refs):
    count = (len(refs) - 2) // 3
    sources, targets, buffers = refs[:count], refs[count : 2 * count], refs[2 * count : 3 * count]
    in_sem, out_sem = refs[3 * count :]
    loads = [pltpu.make_async_copy(sources[i], buffers[i], in_sem.at[i]) for i in range(count)]
    stores = [pltpu.make_async_copy(buffers[i], targets[i], out_sem.at[i]) for i in range(count)]
    for copy in loads:
        copy.start()
    for load, store in zip(loads, stores):
        load.wait()
        store.start()
    for copy in stores:
        copy.wait()


def local(query_proj, key_proj, value_proj, filters, w_out, cotangent):
    positions, channels = query_proj.shape[1:]
    features = w_out.shape[1] // SEQ
    half_rows = features // DP
    factor = 1.0 / math.sqrt(DP * LENGTH)
    one, back, two, twiddle = (jnp.asarray(table) for table in tables())
    stream = jax.ShapeDtypeStruct((positions, channels), BF16)
    anywhere = pl.BlockSpec(memory_space=pl.ANY)
    chunks = pltpu.VMEM((GROUP, 2 * CH, LANES), BF16)
    half_chunks = pltpu.VMEM((SEQ, 2 * CH, LANES), BF16)
    stream_buffer = pltpu.VMEM((positions, channels), BF16)
    wide_buffer = pltpu.VMEM((positions, channels), F32)
    cut = 2
    lanes = channels // cut
    dma = pltpu.SemaphoreType.DMA
    out_shape = (
        stream,
        stream,
        stream,
        stream,
        jax.ShapeDtypeStruct((channels, positions), F32),
        jax.ShapeDtypeStruct((features, channels), F32),
    )
    outs = pl.pallas_call(
        functools.partial(kernel, factor),
        out_shape=out_shape,
        in_specs=[anywhere] * 10,
        out_specs=[anywhere] * 6,
        scratch_shapes=[
            stream_buffer, stream_buffer, stream_buffer,
            pltpu.VMEM(filters.shape, F32),
            pltpu.VMEM(w_out.shape, BF16),
            *[pltpu.VMEM(out.shape, out.dtype) for out in out_shape],
            pltpu.VMEM(one.shape, BF16),
            pltpu.VMEM(back.shape, BF16),
            pltpu.VMEM(two.shape, BF16),
            pltpu.VMEM(twiddle.shape, F32),
            chunks, chunks, half_chunks, half_chunks, chunks, chunks,
            chunks, chunks, chunks, chunks, half_chunks, half_chunks, half_chunks,
            pltpu.VMEM((4, positions, channels), BF16),
            pltpu.VMEM((SEQ, DP, half_rows, positions), BF16),
            pltpu.VMEM((SEQ, half_rows, positions), BF16),
            wide_buffer,
            pltpu.VMEM((ROWS, DP * LANES), BF16),
            pltpu.VMEM((DP, ROWS, 2 * LANES), F32),
            pltpu.VMEM((1, ROWS, 2 * LANES), F32),
            pltpu.VMEM((DP, ROWS, 2 * LANES), F32),
            pltpu.VMEM((2 * ROWS, DP * LANES), BF16),
            pltpu.VMEM((2 * ROWS, DP * LANES), BF16),
            stream_buffer, stream_buffer,
            pltpu.VMEM((cut, YN, ZN, half_rows, lanes), BF16),
            pltpu.VMEM((cut, YN - 1, ZN, half_rows, lanes), BF16),
            pltpu.VMEM((cut, ZN, half_rows, lanes), BF16),
            pltpu.VMEM((cut, ZN, half_rows, lanes), BF16),
            pltpu.VMEM((half_rows, channels), F32),
            pltpu.VMEM((half_rows, channels), F32),
            pltpu.VMEM((2, positions, channels), F32),
            pltpu.VMEM((2, positions, channels), F32),
            stream_buffer, stream_buffer,
            wide_buffer,
            dma((10,)), dma((6,)), dma((6,)), dma((6,)), dma((5,)), dma((5,)), dma((4,)), dma((4,)),
            dma((cut, 3)), dma((cut, 3)), dma((cut, 7)), dma((cut, 7)),
        ],
        compiler_params=pltpu.CompilerParams(
            collective_id=0, has_side_effects=True, vmem_limit_bytes=56 * 1024 * 1024
        ),
        cost_estimate=pl.CostEstimate(flops=8_000_000_000, bytes_accessed=12_000_000, transcendentals=0),
    )(query_proj[0], key_proj[0], value_proj[0], filters, w_out, cotangent[0], one, back, two, twiddle)
    outs = pl.pallas_call(
        hand_over,
        out_shape=out_shape,
        in_specs=[anywhere] * 6,
        out_specs=[anywhere] * 6,
        scratch_shapes=[*[pltpu.VMEM(out.shape, out.dtype) for out in out_shape], dma((6,)), dma((6,))],
    )(*outs)
    output, grad_query, grad_key, grad_value, grad_filter, grad_wout = outs
    return (
        output[None],
        grad_query[None],
        grad_key[None],
        grad_value[None],
        grad_filter,
        grad_wout.T,
    )


def solution(mesh):
    stream = P("dp", "ctx", "tp")
    taps = P("tp", "ctx")
    return jax.shard_map(
        local,
        mesh=mesh,
        in_specs=(stream, stream, stream, taps, P("tp", None), stream),
        out_specs=(stream, stream, stream, stream, taps, taps),
        check_vma=False,
    )
```

time: 102 us -> 80.3 us (0.79)
  Pallas kernels: 92.4 us -> 79.6 us
  local copies, waits for them, and re-layouts: 8.3 us -> 0 us
    pallas_call x1 -> x2, Pallas kernels: 92.4 us -> 79.6 us  [the longest x1 77.3 us: local(): pl.pallas_call(functools.partial(kernel, factor), out_shape=out_shape, in...]
    unnamed x10 -> x0, local copies, waits for them, and re-layouts: 8.3 us -> none
where the time goes in v1:
time: 80.3 us; the launch traced here: 80.2 us
  Pallas kernels  79.6 us (99%)
    pallas_call x1, Pallas kernels, local(): pl.pallas_call(functools.partial(kernel, factor), out_shape=out_shape, in...  77.3 us
    pallas_call x1, Pallas kernels, local(): pl.pallas_call(hand_over, out_shape=out_shape, in_specs=[anywhere] * 6, o...  2.29 us

profile of v1, /device:TPU:1, one launch (start us, length us, event | category | flops | bytes accessed | tf_op | source)
XLA Modules:
  0.0 80.2 jit_solution(14865693712951483371)
XLA Ops:
  0.6 77.3 %shard_map.145 = (bf16[256,512]{1,0:T(8,128)(2,1)}, bf16[256,512]{1,0:T(8,128)(2,1)}, bf16[256,512]{1,0:T(8,128)(2,1)}, bf16[256,512]{1,0:T(8,128)(2,1)}, f32[512,256]{1,0:T(8,128)}, /*index=5*/f32[64,512]{1,0:T(8,128)}) custom-call(bf16[256,512]{1,0:T(8,128)(2,1)} %bitcast.9, bf16[256,512]{1,0:T(8,128)(2,1)} %bitcast.10, bf16[256,512]{1,0:T(8,128)(2,1)} %bitcast.11, ...), custom_call_target="tpu_custom_call" | custom-call | flops 8000000000 | bytes 12000000 | tf_op jit(solution)/shard_map/pallas_call | solution.py:474
  77.9 2.3 %shard_map.146 = (bf16[256,512]{1,0:T(8,128)(2,1)}, bf16[256,512]{1,0:T(8,128)(2,1)}, bf16[256,512]{1,0:T(8,128)(2,1)}, bf16[256,512]{1,0:T(8,128)(2,1)}, f32[512,256]{1,0:T(8,128)}, /*index=5*/f32[64,512]{1,0:T(8,128)}) custom-call(bf16[256,512]{1,0:T(8,128)(2,1)} %get-tuple-element.18.refs_0_, bf16[256,512]{1,0:T(8,128)(2,1)} %get-tuple-element.19.refs_1_, ...), custom_call_target="tpu_custom_call" | custom-call | tf_op jit(solution)/shard_map/pallas_call | solution.py:519

commit v2 on v1

--- a/solution.py
+++ b/solution.py
@@ -111,13 +111,13 @@
         copy.start()
         return copy
 
+    lax.fori_loop(1, GROUP, greet, 0, unroll=9)
+    for other in (t_core, t_x):
+        pl.semaphore_signal(barrier, inc=1, device_id={"tp": other}, device_id_type=MESH)
     load_f = load(f_hbm, f_ref, 0)
+    load_cot = load(cot_hbm, cot_all.at[t], 3)
     load_k = load(k_hbm, k_ref, 1)
     load_v = load(v_hbm, v_ref, 2)
-    load_cot = load(cot_hbm, cot_all.at[t], 3)
-    lax.fori_loop(1, GROUP, greet, 0)
-    for other in (t_core, t_x):
-        pl.semaphore_signal(barrier, inc=1, device_id={"tp": other}, device_id_type=MESH)
     load_w = load(w_hbm, w_ref, 4)
     load_q = load(q_hbm, q_ref, 5)
     load_tables = [
@@ -140,10 +140,6 @@
     load_f.wait()
     fil_send[...] = to_chunks(f_ref[pl.ds(pl.multiple_of(d * half, half), half), :])
     fil_recv[j] = fil_send[j]
-    load_k.wait()
-    load_v.wait()
-    mix_send[...] = to_chunks((k_ref[...].astype(F32) * v_ref[...].astype(F32)).T)
-    mix_recv[me] = mix_send[me]
     load_cot.wait()
 
     pl.semaphore_wait(barrier, GROUP + 1)
@@ -185,6 +181,10 @@
         return remote(part, part, send_sem.at[index], recv_sem.at[index], {"tp": t_core})
 
     scatter_same(fil_send, fil_recv, 1)
+    load_k.wait()
+    load_v.wait()
+    mix_send[...] = to_chunks((k_ref[...].astype(F32) * v_ref[...].astype(F32)).T)
+    mix_recv[me] = mix_send[me]
     scatter(mix_send, mix_recv, 0)
 
     width = q_ref.shape[1]
@@ -222,7 +222,7 @@
                 spec[b, rows_of(i), :] = dot(high, two[0]) + dot(low, two[0]) + dot(high, two[1])
             return carry
 
-        lax.fori_loop(0, ROWS // STEP, body, 0)
+        lax.fori_loop(0, ROWS // STEP, body, 0, unroll=True)
 
     def inverse_transform(product, count, send):
         def first(i, carry):
@@ -240,7 +240,7 @@
                 v_lo[rows_of(i, ROWS), lanes] = low
             return carry
 
-        lax.fori_loop(0, ROWS // STEP, first, 0)
+        lax.fori_loop(0, ROWS // STEP, first, 0, unroll=True)
 
         def second(i, carry):
             high, low = v_hi[:, : count * LANES], v_lo[:, : count * LANES]
@@ -253,7 +253,7 @@
                 send[pl.ds(b * SEQ + i * chunks, chunks)] = part
             return carry
 
-        lax.fori_loop(0, ROWS // STEP, second, 0)
+        lax.fori_loop(0, ROWS // STEP, second, 0, unroll=True)
 
     def pair(ref, b, rows):
         return ref[b, rows, :LANES], ref[b, rows, LANES:]
@@ -290,6 +290,13 @@
     cot_x.wait_recv()
     forward = tp_copy(cot_all.at[t_x], cot_all.at[t_x], 2, t_core)
     forward.start()
+
+    def cot_pair(x_index, index):
+        blocks = pl.ds(x_index * (SEQ // 2), SEQ // 2)
+        return dp_copy(cot_t.at[blocks, 1 - d], cot_p.at[blocks], index)
+
+    cot_pairs = [cot_pair(hi_x, 0), cot_pair(1 - hi_x, 1)]
+    cot_pairs[0].start()
     gg[...] += grad_part(t_x)
     load_q.wait()
     forward.wait_recv()
@@ -300,8 +307,7 @@
     scatter(gc_send, gc_recv, 2, 1, GROUP // 2)
     turn(t_x)
     turn(t_far)
-    cot_pair = dp_copy(cot_t.at[:, 1 - d], cot_p, 0)
-    cot_pair.start()
+    cot_pairs[1].start()
 
     whole(mix_recv, 0).wait_recv()
     forward_transform(mix_recv, DP, spec_m)
@@ -310,45 +316,41 @@
     scatter(conv_send, conv_recv, 3)
     scatter(gc_send, gc_recv, 2, GROUP // 2, GROUP)
 
+    cut = gated.shape[0]
+    lanes = gated.shape[2]
+    sources = GROUP // cut
+    gated_pairs = [dp_copy(gated.at[c], gated_p.at[c], 2 + c) for c in range(cut)]
     whole(conv_recv, 3).wait_recv()
-    conv = from_chunks(conv_recv).T
-    gated[...] = (q_ref[...].astype(F32) * conv).astype(BF16)
-    gated_pair = dp_copy(gated, gated_p, 1)
-    gated_pair.start()
-    gq_ref[...] = (gg[...] * conv).astype(BF16)
+    for c in range(cut):
+        cols = slice(c * lanes, (c + 1) * lanes)
+        conv = from_chunks(conv_recv.at[pl.ds(c * sources, sources)]).T
+        gated[c] = (q_ref[:, cols].astype(F32) * conv).astype(BF16)
+        gated_pairs[c].start()
+        gq_ref[:, cols] = (gg[:, cols] * conv).astype(BF16)
     stores = [store(gq_ref, gq_hbm, 1)]
 
     def partial(o):
-        return dot(gated[...], w_ref[:, pl.ds(pl.multiple_of(o * width, width), width)])
+        rows = jnp.concatenate([gated[c] for c in range(cut)], axis=1)
+        return dot(rows, w_ref[:, pl.ds(pl.multiple_of(o * width, width), width)])
 
     core_send[0] = partial(t_far)
     core_send[1] = partial(t_core)
     core_copy = tp_copy(core_send, core_recv, 3, t_core)
     core_copy.start()
 
-    whole(gc_recv, 2).wait_recv()
-    forward_transform(gc_recv, DP, spec_g)
-    inverse_transform(grad_product, DP, gm_send)
-    gm_recv[me] = gm_send[me]
-    scatter(gm_send, gm_recv, 4)
-    inverse_transform(taps_product, 1, fg_send)
-    fg_recv[j] = fg_send[j]
-    scatter_same(fg_send, fg_recv, 5)
-
-    cot_pair.wait_recv()
-    gated_pair.wait_recv()
-    chunks = w_send.shape[0]
-    lanes = width // chunks
+    for copy in cot_pairs:
+        copy.wait_recv()
     planes = ZN // 2
     y_copies = []
-    for c in range(chunks):
-        cols = slice(c * lanes, (c + 1) * lanes)
-
-        def weight(i, carry, c=c, cols=cols):
+
+    def weights(c):
+        gated_pairs[c].wait_recv()
+
+        def weight(i, carry):
             blocks = pl.ds(i * planes * YN, planes * YN)
             mine = cot_t[blocks, d].reshape(planes * YN * half_rows, positions)
             other = cot_p[blocks].reshape(planes * YN * half_rows, positions)
-            term = dot(mine, gated[:, cols]) + dot(other, gated_p[:, cols])
+            term = dot(mine, gated[c]) + dot(other, gated_p[c])
             term = term.astype(BF16).reshape(planes, YN, half_rows, lanes)
             for to in range(YN):
                 w_send[c, to, pl.ds(i * planes, planes)] = term[:, to]
@@ -363,6 +365,19 @@
             )
             copy.start()
             y_copies.append(copy)
+
+    for c in range(cut // 2):
+        weights(c)
+    whole(gc_recv, 2).wait_recv()
+    forward_transform(gc_recv, DP, spec_g)
+    inverse_transform(grad_product, DP, gm_send)
+    gm_recv[me] = gm_send[me]
+    scatter(gm_send, gm_recv, 4)
+    for c in range(cut // 2, cut):
+        weights(c)
+    inverse_transform(taps_product, 1, fg_send)
+    fg_recv[j] = fg_send[j]
+    scatter_same(fg_send, fg_recv, 5)
 
     other_x = partial(t_x)
     own[...] = partial(t)
@@ -390,42 +405,42 @@
             copy.start()
             z_copies.append(copy)
 
-    reduce_y(0)
+    for c in range(cut - 1):
+        reduce_y(c)
     whole(gm_recv, 4).wait_recv()
     grad_mixed = from_chunks(gm_recv).T
     gk_ref[...] = (grad_mixed * v_ref[...].astype(F32)).astype(BF16)
     gv_ref[...] = (grad_mixed * k_ref[...].astype(F32)).astype(BF16)
     stores += [store(gk_ref, gk_hbm, 2), store(gv_ref, gv_hbm, 3)]
+    reduce_y(cut - 1)
     whole(fg_recv, 5).wait_recv()
-    fg_pair = dp_copy(fg_recv, fg_part, 2)
+    fg_pair = dp_copy(fg_recv, fg_part, 2 + cut)
     fg_pair.start()
-    for c in range(1, chunks):
-        reduce_y(c)
     x_copy.wait_recv()
     out_ref[...] = (own[...] + core_recv[1] + x_recv[...].astype(F32)).astype(BF16)
     stores.append(store(out_ref, out_hbm, 0))
     gf_ref[pl.ds(pl.multiple_of(d * half, half), half), :] = from_chunks(fg_recv) * factor
-    fg_pair.wait_recv()
-    gf_ref[pl.ds(pl.multiple_of((1 - d) * half, half), half), :] = from_chunks(fg_part) * factor
-    stores.append(store(gf_ref, gf_hbm, 4))
-
-    for c in range(chunks):
+
+    for c in range(cut):
         for copy in z_copies[c * (ZN - 1) : (c + 1) * (ZN - 1)]:
             copy.wait_recv()
         value = z_recv[c, 0].astype(F32)
         for slot in range(1, ZN):
             value += z_recv[c, slot].astype(F32)
         d_send[:, c * lanes : (c + 1) * lanes] = value * factor
-    d_copy = dp_copy(d_send, d_recv, 3)
+    d_copy = dp_copy(d_send, d_recv, 3 + cut)
     d_copy.start()
+    fg_pair.wait_recv()
+    gf_ref[pl.ds(pl.multiple_of((1 - d) * half, half), half), :] = from_chunks(fg_part) * factor
+    stores.append(store(gf_ref, gf_hbm, 4))
     gw_ref[pl.ds(pl.multiple_of(d * half_rows, half_rows), half_rows), :] = d_send[...]
     d_copy.wait_recv()
     gw_ref[pl.ds(pl.multiple_of((1 - d) * half_rows, half_rows), half_rows), :] = d_recv[...]
     stores.append(store(gw_ref, gw_hbm, 5))
 
-    for copy in (cot_core, cot_x, forward, core_copy, x_copy, cot_pair, gated_pair, fg_pair, d_copy):
+    for copy in (cot_core, cot_x, forward, core_copy, x_copy, fg_pair, d_copy):
         copy.wait_send()
-    for copy in y_copies + z_copies:
+    for copy in cot_pairs + gated_pairs + y_copies + z_copies:
         copy.wait_send()
     for index, ref in enumerate((mix_send, fil_send, gc_send, conv_send, gm_send, fg_send)):
         whole(ref, index).wait_send()
@@ -460,8 +475,8 @@
     half_chunks = pltpu.VMEM((SEQ, 2 * CH, LANES), BF16)
     stream_buffer = pltpu.VMEM((positions, channels), BF16)
     wide_buffer = pltpu.VMEM((positions, channels), F32)
-    cut = 2
-    lanes = channels // cut
+    cut = channels // LANES
+    lanes = LANES
     dma = pltpu.SemaphoreType.DMA
     out_shape = (
         stream,
@@ -497,7 +512,8 @@
             pltpu.VMEM((DP, ROWS, 2 * LANES), F32),
             pltpu.VMEM((2 * ROWS, DP * LANES), BF16),
             pltpu.VMEM((2 * ROWS, DP * LANES), BF16),
-            stream_buffer, stream_buffer,
+            pltpu.VMEM((cut, positions, lanes), BF16),
+            pltpu.VMEM((cut, positions, lanes), BF16),
             pltpu.VMEM((cut, YN, ZN, half_rows, lanes), BF16),
             pltpu.VMEM((cut, YN - 1, ZN, half_rows, lanes), BF16),
             pltpu.VMEM((cut, ZN, half_rows, lanes), BF16),
@@ -508,7 +524,7 @@
             pltpu.VMEM((2, positions, channels), F32),
             stream_buffer, stream_buffer,
             wide_buffer,
-            dma((10,)), dma((6,)), dma((6,)), dma((6,)), dma((5,)), dma((5,)), dma((4,)), dma((4,)),
+            dma((10,)), dma((6,)), dma((6,)), dma((6,)), dma((5,)), dma((5,)), dma((4 + cut,)), dma((4 + cut,)),
             dma((cut, 3)), dma((cut, 3)), dma((cut, 7)), dma((cut, 7)),
         ],
         compiler_params=pltpu.CompilerParams(

time: 80.3 us -> 72.3 us (0.900)
  Pallas kernels: 79.6 us -> 71.4 us
    pallas_call x1, Pallas kernels: 77.3 us -> 69.2 us  [local(): pl.pallas_call(functools.partial(kernel, factor), out_shape=out_shape, in...]
where the time goes in v2:
time: 72.3 us; the launch traced here: 72.1 us
  Pallas kernels  71.4 us (99%)
    pallas_call x1, Pallas kernels, local(): pl.pallas_call(functools.partial(kernel, factor), out_shape=out_shape, in...  69.2 us
    pallas_call x1, Pallas kernels, local(): pl.pallas_call(hand_over, out_shape=out_shape, in_specs=[anywhere] * 6, o...  2.29 us

profile of v2, /device:TPU:1, one launch (start us, length us, event | category | flops | bytes accessed | tf_op | source)
XLA Modules:
  0.0 72.1 jit_solution(1004696287443391760)
XLA Ops:
  0.6 69.2 %shard_map.145 = (bf16[256,512]{1,0:T(8,128)(2,1)}, bf16[256,512]{1,0:T(8,128)(2,1)}, bf16[256,512]{1,0:T(8,128)(2,1)}, bf16[256,512]{1,0:T(8,128)(2,1)}, f32[512,256]{1,0:T(8,128)}, /*index=5*/f32[64,512]{1,0:T(8,128)}) custom-call(bf16[256,512]{1,0:T(8,128)(2,1)} %bitcast.9, bf16[256,512]{1,0:T(8,128)(2,1)} %bitcast.10, bf16[256,512]{1,0:T(8,128)(2,1)} %bitcast.11, ...), custom_call_target="tpu_custom_call" | custom-call | flops 8000000000 | bytes 12000000 | tf_op jit(solution)/shard_map/pallas_call | solution.py:489
  69.8 2.3 %shard_map.146 = (bf16[256,512]{1,0:T(8,128)(2,1)}, bf16[256,512]{1,0:T(8,128)(2,1)}, bf16[256,512]{1,0:T(8,128)(2,1)}, bf16[256,512]{1,0:T(8,128)(2,1)}, f32[512,256]{1,0:T(8,128)}, /*index=5*/f32[64,512]{1,0:T(8,128)}) custom-call(bf16[256,512]{1,0:T(8,128)(2,1)} %get-tuple-element.18.refs_0_, bf16[256,512]{1,0:T(8,128)(2,1)} %get-tuple-element.19.refs_1_, ...), custom_call_target="tpu_custom_call" | custom-call | tf_op jit(solution)/shard_map/pallas_call | solution.py:535

commit v3 on v2

--- a/solution.py
+++ b/solution.py
@@ -74,8 +74,8 @@
     mix_send, mix_recv, fil_send, fil_recv, gc_send, gc_recv,
     conv_send, conv_recv, gm_send, gm_recv, fg_send, fg_recv, fg_part,
     cot_all, cot_t, cot_p, gg, xcat, spec_m, spec_f, spec_g, v_hi, v_lo,
-    gated, gated_p, w_send, w_recv, z_send, z_recv, d_send, d_recv,
-    core_send, core_recv, x_send, x_recv, own,
+    gated, gated_p, w_send, w_recv, z_send, z_recv, first_recv, last_send, last_recv, d_send, d_recv,
+    core_send, core_recv, x_send, x_recv, own, across,
     load_sem, store_sem, send_sem, recv_sem, tp_send, tp_recv, dp_send, dp_recv,
     y_ssem, y_rsem, z_ssem, z_rsem,
 ):
@@ -206,14 +206,17 @@
     def rows_of(i, base=0):
         return pl.ds(pl.multiple_of(base + i * STEP, STEP), STEP)
 
-    def forward_transform(recv, count, spec):
+    def forward_transform(recv, count, spec, fine=True):
         for b in range(count):
             xcat[:, b * LANES : (b + 1) * LANES] = recv[b * SEQ : (b + 1) * SEQ].reshape(ROWS, LANES)
 
         def body(i, carry):
             x = xcat[:, : count * LANES]
-            real = dot(one[0, rows_of(i), :], x) + dot(one[1, rows_of(i), :], x)
-            imag = dot(one[0, rows_of(i, ROWS), :], x) + dot(one[1, rows_of(i, ROWS), :], x)
+            real = dot(one[0, rows_of(i), :], x)
+            imag = dot(one[0, rows_of(i, ROWS), :], x)
+            if fine:
+                real += dot(one[1, rows_of(i), :], x)
+                imag += dot(one[1, rows_of(i, ROWS), :], x)
             c, s = tw[0, rows_of(i), :], tw[1, rows_of(i), :]
             for b in range(count):
                 re = real[:, b * LANES : (b + 1) * LANES]
@@ -224,7 +227,7 @@
 
         lax.fori_loop(0, ROWS // STEP, body, 0, unroll=True)
 
-    def inverse_transform(product, count, send):
+    def inverse_transform(product, count, send, fine=True, sent=None):
         def first(i, carry):
             c, s = tw[0, rows_of(i), :], tw[1, rows_of(i), :]
             for b in range(count):
@@ -242,18 +245,37 @@
 
         lax.fori_loop(0, ROWS // STEP, first, 0, unroll=True)
 
-        def second(i, carry):
+        chunks = STEP // (2 * CH)
+        for i in range(ROWS // STEP):
             high, low = v_hi[:, : count * LANES], v_lo[:, : count * LANES]
             table = back[0, rows_of(i), :]
-            result = dot(table, high) + dot(table, low) + dot(back[1, rows_of(i), :], high)
+            result = dot(table, high) + dot(table, low)
+            if fine:
+                result += dot(back[1, rows_of(i), :], high)
             result = (result * (1.0 / LENGTH)).astype(BF16)
-            chunks = STEP // (2 * CH)
             for b in range(count):
                 part = result[:, b * LANES : (b + 1) * LANES].reshape(chunks, 2 * CH, LANES)
                 send[pl.ds(b * SEQ + i * chunks, chunks)] = part
-            return carry
-
-        lax.fori_loop(0, ROWS // STEP, second, 0, unroll=True)
+            if sent is not None:
+                sent(i * chunks, chunks)
+
+    def scatter_part(src, dst, index):
+        def part(base, length):
+            def start(i, carry):
+                sequence = lax.rem(d + 1 + i // length, DP)
+                position = base + lax.rem(i + j, length)
+                p = sequence * SEQ + position
+
+                @pl.when(p != me)
+                def _():
+                    device = {"dp": sequence, "ctx": position}
+                    remote(src.at[p], dst.at[me], send_sem.at[index], recv_sem.at[index], device).start()
+
+                return carry
+
+            lax.fori_loop(0, DP * length, start, 0)
+
+        return part
 
     def pair(ref, b, rows):
         return ref[b, rows, :LANES], ref[b, rows, LANES:]
@@ -298,23 +320,21 @@
     cot_pairs = [cot_pair(hi_x, 0), cot_pair(1 - hi_x, 1)]
     cot_pairs[0].start()
     gg[...] += grad_part(t_x)
+    turn(t_x)
+    forward.wait_recv()
+    turn(t_far)
+    cot_pairs[1].start()
+
+    whole(mix_recv, 0).wait_recv()
+    forward_transform(mix_recv, DP, spec_m)
+    inverse_transform(conv_product, DP, conv_send, sent=scatter_part(conv_send, conv_recv, 3))
+    conv_recv[me] = conv_send[me]
     load_q.wait()
-    forward.wait_recv()
     total = gg[...] + grad_part(t_far)
     gg[...] = total
     gc_send[...] = to_chunks((total * q_ref[...].astype(F32)).T)
     gc_recv[me] = gc_send[me]
-    scatter(gc_send, gc_recv, 2, 1, GROUP // 2)
-    turn(t_x)
-    turn(t_far)
-    cot_pairs[1].start()
-
-    whole(mix_recv, 0).wait_recv()
-    forward_transform(mix_recv, DP, spec_m)
-    inverse_transform(conv_product, DP, conv_send)
-    conv_recv[me] = conv_send[me]
-    scatter(conv_send, conv_recv, 3)
-    scatter(gc_send, gc_recv, 2, GROUP // 2, GROUP)
+    scatter(gc_send, gc_recv, 2)
 
     cut = gated.shape[0]
     lanes = gated.shape[2]
@@ -337,11 +357,38 @@
     core_send[1] = partial(t_core)
     core_copy = tp_copy(core_send, core_recv, 3, t_core)
     core_copy.start()
+    across[...] = partial(t_x)
+    own[...] = partial(t)
 
     for copy in cot_pairs:
         copy.wait_recv()
     planes = ZN // 2
-    y_copies = []
+    y_copies = [[] for _ in range(cut)]
+    z_copies = [[] for _ in range(cut)]
+
+    def along_y(c, src, dst):
+        for step in (2, 1, 3):
+            to = lax.rem(y + step, YN)
+            copy = remote(
+                src(to), dst(step), y_ssem.at[c, step - 1], y_rsem.at[c, step - 1], {"ctx": z * YN + to}
+            )
+            copy.start()
+            y_copies[c].append(copy)
+
+    def along_z(c, src, dst):
+        for step in (4, 3, 5, 2, 6, 1, 7):
+            to = lax.rem(z + step, ZN)
+            copy = remote(
+                src(to), dst(step), z_ssem.at[c, step - 1], z_rsem.at[c, step - 1], {"ctx": to * YN + y}
+            )
+            copy.start()
+            z_copies[c].append(copy)
+
+    def sum_of(parts):
+        value = parts[0].astype(F32)
+        for part in parts[1:]:
+            value += part.astype(F32)
+        return value
 
     def weights(c):
         gated_pairs[c].wait_recv()
@@ -357,62 +404,51 @@
             return carry
 
         lax.fori_loop(0, 2, weight, 0)
-        for step in (2, 1, 3):
-            to = lax.rem(y + step, YN)
-            copy = remote(
-                w_send.at[c, to], w_recv.at[c, step - 1], y_ssem.at[c, step - 1], y_rsem.at[c, step - 1],
-                {"ctx": z * YN + to},
-            )
-            copy.start()
-            y_copies.append(copy)
-
-    for c in range(cut // 2):
+        if c == 0:
+            first_recv[z] = w_send[c, :, z]
+            along_z(c, lambda to: w_send.at[c, :, to], lambda step: first_recv.at[z])
+        else:
+            along_y(c, lambda to: w_send.at[c, to], lambda step: w_recv.at[c - 1, step - 1])
+
+    for c in range(cut - 1):
         weights(c)
+    core_copy.wait_recv()
+    x_send[...] = (across[...] + core_recv[0]).astype(BF16)
+    x_copy = tp_copy(x_send, x_recv, 4, t_x)
+    x_copy.start()
     whole(gc_recv, 2).wait_recv()
-    forward_transform(gc_recv, DP, spec_g)
-    inverse_transform(grad_product, DP, gm_send)
+    forward_transform(gc_recv, DP, spec_g, False)
+    inverse_transform(grad_product, DP, gm_send, False, scatter_part(gm_send, gm_recv, 4))
     gm_recv[me] = gm_send[me]
-    scatter(gm_send, gm_recv, 4)
-    for c in range(cut // 2, cut):
-        weights(c)
-    inverse_transform(taps_product, 1, fg_send)
+    weights(cut - 1)
+    inverse_transform(taps_product, 1, fg_send, False)
     fg_recv[j] = fg_send[j]
     scatter_same(fg_send, fg_recv, 5)
 
-    other_x = partial(t_x)
-    own[...] = partial(t)
-    core_copy.wait_recv()
-    x_send[...] = (other_x + core_recv[0]).astype(BF16)
-    x_copy = tp_copy(x_send, x_recv, 4, t_x)
-    x_copy.start()
-
-    z_copies = []
+
+    def reduce_z(c):
+        for copy in z_copies[c]:
+            copy.wait_recv()
+        last_send[...] = sum_of([first_recv[slot] for slot in range(ZN)]).astype(BF16)
+        last_recv[y] = last_send[y]
+        along_y(c, lambda to: last_send.at[to], lambda step: last_recv.at[y])
 
     def reduce_y(c):
-        for copy in y_copies[c * 3 : c * 3 + 3]:
+        for copy in y_copies[c]:
             copy.wait_recv()
-        value = w_send[c, y].astype(F32)
-        for slot in range(YN - 1):
-            value += w_recv[c, slot].astype(F32)
-        z_send[c] = value.astype(BF16)
-        z_recv[c, z] = z_send[c, z]
-        for step in (4, 3, 5, 2, 6, 1, 7):
-            to = lax.rem(z + step, ZN)
-            copy = remote(
-                z_send.at[c, to], z_recv.at[c, z], z_ssem.at[c, step - 1], z_rsem.at[c, step - 1],
-                {"ctx": to * YN + y},
-            )
-            copy.start()
-            z_copies.append(copy)
-
-    for c in range(cut - 1):
+        value = sum_of([w_send[c, y]] + [w_recv[c - 1, slot] for slot in range(YN - 1)])
+        z_send[c - 1] = value.astype(BF16)
+        z_recv[c - 1, z] = z_send[c - 1, z]
+        along_z(c, lambda to: z_send.at[c - 1, to], lambda step: z_recv.at[c - 1, z])
+
+    reduce_z(0)
+    for c in range(1, cut):
         reduce_y(c)
     whole(gm_recv, 4).wait_recv()
     grad_mixed = from_chunks(gm_recv).T
     gk_ref[...] = (grad_mixed * v_ref[...].astype(F32)).astype(BF16)
     gv_ref[...] = (grad_mixed * k_ref[...].astype(F32)).astype(BF16)
     stores += [store(gk_ref, gk_hbm, 2), store(gv_ref, gv_hbm, 3)]
-    reduce_y(cut - 1)
     whole(fg_recv, 5).wait_recv()
     fg_pair = dp_copy(fg_recv, fg_part, 2 + cut)
     fg_pair.start()
@@ -421,26 +457,29 @@
     stores.append(store(out_ref, out_hbm, 0))
     gf_ref[pl.ds(pl.multiple_of(d * half, half), half), :] = from_chunks(fg_recv) * factor
 
+    d_copies = []
     for c in range(cut):
-        for copy in z_copies[c * (ZN - 1) : (c + 1) * (ZN - 1)]:
+        for copy in y_copies[c] if c == 0 else z_copies[c]:
             copy.wait_recv()
-        value = z_recv[c, 0].astype(F32)
-        for slot in range(1, ZN):
-            value += z_recv[c, slot].astype(F32)
-        d_send[:, c * lanes : (c + 1) * lanes] = value * factor
-    d_copy = dp_copy(d_send, d_recv, 3 + cut)
-    d_copy.start()
+        slots = [last_recv[i] for i in range(YN)] if c == 0 else [z_recv[c - 1, i] for i in range(ZN)]
+        value = sum_of(slots)
+        d_send[c] = value * factor
+        d_copy = dp_copy(d_send.at[c], d_recv.at[c], 3 + cut + c)
+        d_copy.start()
+        d_copies.append(d_copy)
     fg_pair.wait_recv()
     gf_ref[pl.ds(pl.multiple_of((1 - d) * half, half), half), :] = from_chunks(fg_part) * factor
     stores.append(store(gf_ref, gf_hbm, 4))
-    gw_ref[pl.ds(pl.multiple_of(d * half_rows, half_rows), half_rows), :] = d_send[...]
-    d_copy.wait_recv()
-    gw_ref[pl.ds(pl.multiple_of((1 - d) * half_rows, half_rows), half_rows), :] = d_recv[...]
+    for c in range(cut):
+        cols = slice(c * lanes, (c + 1) * lanes)
+        gw_ref[pl.ds(pl.multiple_of(d * half_rows, half_rows), half_rows), cols] = d_send[c]
+        d_copies[c].wait_recv()
+        gw_ref[pl.ds(pl.multiple_of((1 - d) * half_rows, half_rows), half_rows), cols] = d_recv[c]
     stores.append(store(gw_ref, gw_hbm, 5))
 
-    for copy in (cot_core, cot_x, forward, core_copy, x_copy, fg_pair, d_copy):
+    for copy in (cot_core, cot_x, forward, core_copy, x_copy, fg_pair):
         copy.wait_send()
-    for copy in cot_pairs + gated_pairs + y_copies + z_copies:
+    for copy in cot_pairs + gated_pairs + sum(y_copies + z_copies, []) + d_copies:
         copy.wait_send()
     for index, ref in enumerate((mix_send, fil_send, gc_send, conv_send, gm_send, fg_send)):
         whole(ref, index).wait_send()
@@ -515,16 +554,19 @@
             pltpu.VMEM((cut, positions, lanes), BF16),
             pltpu.VMEM((cut, positions, lanes), BF16),
             pltpu.VMEM((cut, YN, ZN, half_rows, lanes), BF16),
-            pltpu.VMEM((cut, YN - 1, ZN, half_rows, lanes), BF16),
-            pltpu.VMEM((cut, ZN, half_rows, lanes), BF16),
-            pltpu.VMEM((cut, ZN, half_rows, lanes), BF16),
-            pltpu.VMEM((half_rows, channels), F32),
-            pltpu.VMEM((half_rows, channels), F32),
+            pltpu.VMEM((cut - 1, YN - 1, ZN, half_rows, lanes), BF16),
+            pltpu.VMEM((cut - 1, ZN, half_rows, lanes), BF16),
+            pltpu.VMEM((cut - 1, ZN, half_rows, lanes), BF16),
+            pltpu.VMEM((ZN, YN, half_rows, lanes), BF16),
+            pltpu.VMEM((YN, half_rows, lanes), BF16),
+            pltpu.VMEM((YN, half_rows, lanes), BF16),
+            pltpu.VMEM((cut, half_rows, lanes), F32),
+            pltpu.VMEM((cut, half_rows, lanes), F32),
             pltpu.VMEM((2, positions, channels), F32),
             pltpu.VMEM((2, positions, channels), F32),
             stream_buffer, stream_buffer,
-            wide_buffer,
-            dma((10,)), dma((6,)), dma((6,)), dma((6,)), dma((5,)), dma((5,)), dma((4 + cut,)), dma((4 + cut,)),
+            wide_buffer, wide_buffer,
+            dma((10,)), dma((6,)), dma((6,)), dma((6,)), dma((5,)), dma((5,)), dma((3 + 2 * cut,)), dma((3 + 2 * cut,)),
             dma((cut, 3)), dma((cut, 3)), dma((cut, 7)), dma((cut, 7)),
         ],
         compiler_params=pltpu.CompilerParams(

time: 72.3 us -> 73 us (level)
  Pallas kernels: 71.4 us -> 72.3 us
    pallas_call x1, Pallas kernels: 69.2 us -> 70 us  [local(): pl.pallas_call(functools.partial(kernel, factor), out_shape=out_shape, in...]
where the time goes in v3:
time: 73 us; the launch traced here: 72.9 us
  Pallas kernels  72.3 us (99%)
    pallas_call x1, Pallas kernels, local(): pl.pallas_call(functools.partial(kernel, factor), out_shape=out_shape, in...  70 us
    pallas_call x1, Pallas kernels, local(): pl.pallas_call(hand_over, out_shape=out_shape, in_specs=[anywhere] * 6, o...  2.29 us

profile of v3, /device:TPU:1, one launch (start us, length us, event | category | flops | bytes accessed | tf_op | source)
XLA Modules:
  0.0 72.9 jit_solution(11259329966247318071)
XLA Ops:
  0.6 70.0 %shard_map.145 = (bf16[256,512]{1,0:T(8,128)(2,1)}, bf16[256,512]{1,0:T(8,128)(2,1)}, bf16[256,512]{1,0:T(8,128)(2,1)}, bf16[256,512]{1,0:T(8,128)(2,1)}, f32[512,256]{1,0:T(8,128)}, /*index=5*/f32[64,512]{1,0:T(8,128)}) custom-call(bf16[256,512]{1,0:T(8,128)(2,1)} %bitcast.9, bf16[256,512]{1,0:T(8,128)(2,1)} %bitcast.10, bf16[256,512]{1,0:T(8,128)(2,1)} %bitcast.11, ...), custom_call_target="tpu_custom_call" | custom-call | flops 8000000000 | bytes 12000000 | tf_op jit(solution)/shard_map/pallas_call | solution.py:528
  70.6 2.3 %shard_map.146 = (bf16[256,512]{1,0:T(8,128)(2,1)}, bf16[256,512]{1,0:T(8,128)(2,1)}, bf16[256,512]{1,0:T(8,128)(2,1)}, bf16[256,512]{1,0:T(8,128)(2,1)}, f32[512,256]{1,0:T(8,128)}, /*index=5*/f32[64,512]{1,0:T(8,128)}) custom-call(bf16[256,512]{1,0:T(8,128)(2,1)} %get-tuple-element.18.refs_0_, bf16[256,512]{1,0:T(8,128)(2,1)} %get-tuple-element.19.refs_1_, ...), custom_call_target="tpu_custom_call" | custom-call | tf_op jit(solution)/shard_map/pallas_call | solution.py:577

commit v4 on v2

--- a/solution.py
+++ b/solution.py
@@ -75,7 +75,7 @@
     conv_send, conv_recv, gm_send, gm_recv, fg_send, fg_recv, fg_part,
     cot_all, cot_t, cot_p, gg, xcat, spec_m, spec_f, spec_g, v_hi, v_lo,
     gated, gated_p, w_send, w_recv, z_send, z_recv, d_send, d_recv,
-    core_send, core_recv, x_send, x_recv, own,
+    core_send, core_recv, x_send, x_recv, own, across,
     load_sem, store_sem, send_sem, recv_sem, tp_send, tp_recv, dp_send, dp_recv,
     y_ssem, y_rsem, z_ssem, z_rsem,
 ):
@@ -298,14 +298,8 @@
     cot_pairs = [cot_pair(hi_x, 0), cot_pair(1 - hi_x, 1)]
     cot_pairs[0].start()
     gg[...] += grad_part(t_x)
-    load_q.wait()
+    turn(t_x)
     forward.wait_recv()
-    total = gg[...] + grad_part(t_far)
-    gg[...] = total
-    gc_send[...] = to_chunks((total * q_ref[...].astype(F32)).T)
-    gc_recv[me] = gc_send[me]
-    scatter(gc_send, gc_recv, 2, 1, GROUP // 2)
-    turn(t_x)
     turn(t_far)
     cot_pairs[1].start()
 
@@ -314,7 +308,12 @@
     inverse_transform(conv_product, DP, conv_send)
     conv_recv[me] = conv_send[me]
     scatter(conv_send, conv_recv, 3)
-    scatter(gc_send, gc_recv, 2, GROUP // 2, GROUP)
+    load_q.wait()
+    total = gg[...] + grad_part(t_far)
+    gg[...] = total
+    gc_send[...] = to_chunks((total * q_ref[...].astype(F32)).T)
+    gc_recv[me] = gc_send[me]
+    scatter(gc_send, gc_recv, 2)
 
     cut = gated.shape[0]
     lanes = gated.shape[2]
@@ -337,6 +336,8 @@
     core_send[1] = partial(t_core)
     core_copy = tp_copy(core_send, core_recv, 3, t_core)
     core_copy.start()
+    across[...] = partial(t_x)
+    own[...] = partial(t)
 
     for copy in cot_pairs:
         copy.wait_recv()
@@ -366,25 +367,22 @@
             copy.start()
             y_copies.append(copy)
 
-    for c in range(cut // 2):
+    for c in range(cut - 1):
         weights(c)
+    core_copy.wait_recv()
+    x_send[...] = (across[...] + core_recv[0]).astype(BF16)
+    x_copy = tp_copy(x_send, x_recv, 4, t_x)
+    x_copy.start()
     whole(gc_recv, 2).wait_recv()
     forward_transform(gc_recv, DP, spec_g)
     inverse_transform(grad_product, DP, gm_send)
     gm_recv[me] = gm_send[me]
     scatter(gm_send, gm_recv, 4)
-    for c in range(cut // 2, cut):
-        weights(c)
+    weights(cut - 1)
     inverse_transform(taps_product, 1, fg_send)
     fg_recv[j] = fg_send[j]
     scatter_same(fg_send, fg_recv, 5)
 
-    other_x = partial(t_x)
-    own[...] = partial(t)
-    core_copy.wait_recv()
-    x_send[...] = (other_x + core_recv[0]).astype(BF16)
-    x_copy = tp_copy(x_send, x_recv, 4, t_x)
-    x_copy.start()
 
     z_copies = []
 
@@ -405,14 +403,13 @@
             copy.start()
             z_copies.append(copy)
 
-    for c in range(cut - 1):
+    for c in range(cut):
         reduce_y(c)
     whole(gm_recv, 4).wait_recv()
     grad_mixed = from_chunks(gm_recv).T
     gk_ref[...] = (grad_mixed * v_ref[...].astype(F32)).astype(BF16)
     gv_ref[...] = (grad_mixed * k_ref[...].astype(F32)).astype(BF16)
     stores += [store(gk_ref, gk_hbm, 2), store(gv_ref, gv_hbm, 3)]
-    reduce_y(cut - 1)
     whole(fg_recv, 5).wait_recv()
     fg_pair = dp_copy(fg_recv, fg_part, 2 + cut)
     fg_pair.start()
@@ -421,26 +418,30 @@
     stores.append(store(out_ref, out_hbm, 0))
     gf_ref[pl.ds(pl.multiple_of(d * half, half), half), :] = from_chunks(fg_recv) * factor
 
+    d_copies = []
     for c in range(cut):
         for copy in z_copies[c * (ZN - 1) : (c + 1) * (ZN - 1)]:
             copy.wait_recv()
         value = z_recv[c, 0].astype(F32)
         for slot in range(1, ZN):
             value += z_recv[c, slot].astype(F32)
-        d_send[:, c * lanes : (c + 1) * lanes] = value * factor
-    d_copy = dp_copy(d_send, d_recv, 3 + cut)
-    d_copy.start()
+        d_send[c] = value * factor
+        d_copy = dp_copy(d_send.at[c], d_recv.at[c], 3 + cut + c)
+        d_copy.start()
+        d_copies.append(d_copy)
     fg_pair.wait_recv()
     gf_ref[pl.ds(pl.multiple_of((1 - d) * half, half), half), :] = from_chunks(fg_part) * factor
     stores.append(store(gf_ref, gf_hbm, 4))
-    gw_ref[pl.ds(pl.multiple_of(d * half_rows, half_rows), half_rows), :] = d_send[...]
-    d_copy.wait_recv()
-    gw_ref[pl.ds(pl.multiple_of((1 - d) * half_rows, half_rows), half_rows), :] = d_recv[...]
+    for c in range(cut):
+        cols = slice(c * lanes, (c + 1) * lanes)
+        gw_ref[pl.ds(pl.multiple_of(d * half_rows, half_rows), half_rows), cols] = d_send[c]
+        d_copies[c].wait_recv()
+        gw_ref[pl.ds(pl.multiple_of((1 - d) * half_rows, half_rows), half_rows), cols] = d_recv[c]
     stores.append(store(gw_ref, gw_hbm, 5))
 
-    for copy in (cot_core, cot_x, forward, core_copy, x_copy, fg_pair, d_copy):
+    for copy in (cot_core, cot_x, forward, core_copy, x_copy, fg_pair):
         copy.wait_send()
-    for copy in cot_pairs + gated_pairs + y_copies + z_copies:
+    for copy in cot_pairs + gated_pairs + y_copies + z_copies + d_copies:
         copy.wait_send()
     for index, ref in enumerate((mix_send, fil_send, gc_send, conv_send, gm_send, fg_send)):
         whole(ref, index).wait_send()
@@ -518,13 +519,13 @@
             pltpu.VMEM((cut, YN - 1, ZN, half_rows, lanes), BF16),
             pltpu.VMEM((cut, ZN, half_rows, lanes), BF16),
             pltpu.VMEM((cut, ZN, half_rows, lanes), BF16),
-            pltpu.VMEM((half_rows, channels), F32),
-            pltpu.VMEM((half_rows, channels), F32),
+            pltpu.VMEM((cut, half_rows, lanes), F32),
+            pltpu.VMEM((cut, half_rows, lanes), F32),
             pltpu.VMEM((2, positions, channels), F32),
             pltpu.VMEM((2, positions, channels), F32),
             stream_buffer, stream_buffer,
-            wide_buffer,
-            dma((10,)), dma((6,)), dma((6,)), dma((6,)), dma((5,)), dma((5,)), dma((4 + cut,)), dma((4 + cut,)),
+            wide_buffer, wide_buffer,
+            dma((10,)), dma((6,)), dma((6,)), dma((6,)), dma((5,)), dma((5,)), dma((3 + 2 * cut,)), dma((3 + 2 * cut,)),
             dma((cut, 3)), dma((cut, 3)), dma((cut, 7)), dma((cut, 7)),
         ],
         compiler_params=pltpu.CompilerParams(

time: 72.3 us -> 71.4 us (0.988); the launches traced: 72.1 us -> 70.4 us
  Pallas kernels: 71.4 us -> 69.7 us
    pallas_call x1, Pallas kernels: 69.2 us -> 67.4 us  [local(): pl.pallas_call(functools.partial(kernel, factor), out_shape=out_shape, in...]
where the time goes in v4:
time: 71.4 us; the launch traced here: 70.4 us
  Pallas kernels  69.7 us (98%)
    pallas_call x1, Pallas kernels, local(): pl.pallas_call(functools.partial(kernel, factor), out_shape=out_shape, in...  67.4 us
    pallas_call x1, Pallas kernels, local(): pl.pallas_call(hand_over, out_shape=out_shape, in_specs=[anywhere] * 6, o...  2.29 us

profile of v4, /device:TPU:1, one launch (start us, length us, event | category | flops | bytes accessed | tf_op | source)
XLA Modules:
  0.0 70.4 jit_solution(3847207703717248899)
XLA Ops:
  0.6 67.4 %shard_map.145 = (bf16[256,512]{1,0:T(8,128)(2,1)}, bf16[256,512]{1,0:T(8,128)(2,1)}, bf16[256,512]{1,0:T(8,128)(2,1)}, bf16[256,512]{1,0:T(8,128)(2,1)}, f32[512,256]{1,0:T(8,128)}, /*index=5*/f32[64,512]{1,0:T(8,128)}) custom-call(bf16[256,512]{1,0:T(8,128)(2,1)} %bitcast.9, bf16[256,512]{1,0:T(8,128)(2,1)} %bitcast.10, bf16[256,512]{1,0:T(8,128)(2,1)} %bitcast.11, ...), custom_call_target="tpu_custom_call" | custom-call | flops 8000000000 | bytes 12000000 | tf_op jit(solution)/shard_map/pallas_call | solution.py:490
  68.1 2.3 %shard_map.146 = (bf16[256,512]{1,0:T(8,128)(2,1)}, bf16[256,512]{1,0:T(8,128)(2,1)}, bf16[256,512]{1,0:T(8,128)(2,1)}, bf16[256,512]{1,0:T(8,128)(2,1)}, f32[512,256]{1,0:T(8,128)}, /*index=5*/f32[64,512]{1,0:T(8,128)}) custom-call(bf16[256,512]{1,0:T(8,128)(2,1)} %get-tuple-element.18.refs_0_, bf16[256,512]{1,0:T(8,128)(2,1)} %get-tuple-element.19.refs_1_, ...), custom_call_target="tpu_custom_call" | custom-call | tf_op jit(solution)/shard_map/pallas_call | solution.py:536

commit v5 on v4

--- a/solution.py
+++ b/solution.py
@@ -98,7 +98,8 @@
     barrier = pltpu.get_barrier_semaphore()
 
     def greet(i, carry):
-        pl.semaphore_signal(barrier, inc=1, device_id=peer(i)[1], device_id_type=MESH)
+        far_first = lax.rem(i + GROUP // 4 - 2, GROUP - 1) + 1
+        pl.semaphore_signal(barrier, inc=1, device_id=peer(far_first)[1], device_id_type=MESH)
         return carry
 
     def load(src, dst, index):
@@ -357,7 +358,7 @@
                 w_send[c, to, pl.ds(i * planes, planes)] = term[:, to]
             return carry
 
-        lax.fori_loop(0, 2, weight, 0)
+        lax.fori_loop(0, 2, weight, 0, unroll=True)
         for step in (2, 1, 3):
             to = lax.rem(y + step, YN)
             copy = remote(

time: 71.4 us -> 74 us (1.036); the launches traced: 70.4 us -> 73.9 us
  Pallas kernels: 69.7 us -> 73.2 us
    pallas_call x1, Pallas kernels: 67.4 us -> 70.9 us  [local(): pl.pallas_call(functools.partial(kernel, factor), out_shape=out_shape, in...]
where the time goes in v5:
time: 74 us; the launch traced here: 73.9 us
  Pallas kernels  73.2 us (99%)
    pallas_call x1, Pallas kernels, local(): pl.pallas_call(functools.partial(kernel, factor), out_shape=out_shape, in...  70.9 us
    pallas_call x1, Pallas kernels, local(): pl.pallas_call(hand_over, out_shape=out_shape, in_specs=[anywhere] * 6, o...  2.29 us

profile of v5, /device:TPU:1, one launch (start us, length us, event | category | flops | bytes accessed | tf_op | source)
XLA Modules:
  0.0 73.9 jit_solution(5035229564638892852)
XLA Ops:
  0.6 70.9 %shard_map.145 = (bf16[256,512]{1,0:T(8,128)(2,1)}, bf16[256,512]{1,0:T(8,128)(2,1)}, bf16[256,512]{1,0:T(8,128)(2,1)}, bf16[256,512]{1,0:T(8,128)(2,1)}, f32[512,256]{1,0:T(8,128)}, /*index=5*/f32[64,512]{1,0:T(8,128)}) custom-call(bf16[256,512]{1,0:T(8,128)(2,1)} %bitcast.9, bf16[256,512]{1,0:T(8,128)(2,1)} %bitcast.10, bf16[256,512]{1,0:T(8,128)(2,1)} %bitcast.11, ...), custom_call_target="tpu_custom_call" | custom-call | flops 8000000000 | bytes 12000000 | tf_op jit(solution)/shard_map/pallas_call | solution.py:491
  71.6 2.3 %shard_map.146 = (bf16[256,512]{1,0:T(8,128)(2,1)}, bf16[256,512]{1,0:T(8,128)(2,1)}, bf16[256,512]{1,0:T(8,128)(2,1)}, bf16[256,512]{1,0:T(8,128)(2,1)}, f32[512,256]{1,0:T(8,128)}, /*index=5*/f32[64,512]{1,0:T(8,128)}) custom-call(bf16[256,512]{1,0:T(8,128)(2,1)} %get-tuple-element.18.refs_0_, bf16[256,512]{1,0:T(8,128)(2,1)} %get-tuple-element.19.refs_1_, ...), custom_call_target="tpu_custom_call" | custom-call | tf_op jit(solution)/shard_map/pallas_call | solution.py:537
